TPU v7x, 512 devices: a whole 4x8x8 slice. The times are simulated.
512 devices in a mesh: dp: 128 (over z, y, core), tm: 4 (over x).
Axes of the slice: x: 4, y: 8, z: 8, core: 2. Of those that a mesh axis runs over, the one named last changes fastest.
Arguments:
- lengths: int32 [128], P('dp'), may hold values from 17 to 33
- frames: bfloat16 [128, 36, 256, 256], P('dp', 'tm'), may hold values from -6 to 6
- weights: bfloat16 [3, 256, 256], replicated, may hold values from -0.21875 to 0.21875
- cotangent: bfloat16 [128, 36, 256, 256], P('dp', 'tm'), may hold values from -6 to 6
Outputs:
- output: bfloat16 [128, 36, 256, 256], P('dp', 'tm')
- input_grad: bfloat16 [128, 36, 256, 256], P('dp', 'tm')
- weight_grad: float32 [3, 256, 256], replicated
Inputs may be any that keep to these rules, and one draw needn't show every extreme that they name: `lengths`: each clip length lies between half the frame slots less one and the frame slots less three.
All inputs are finite; a program needn't handle non-finite values.
Results may differ from a plain program's by a relative error of at most 0.0049.
Values may be sent and summed in bfloat16 or wider, within the bound.
No kernel may reach another device: no remote copies, remote signals or barrier semaphores. Data moves between devices by JAX's collectives and lax.ppermute only.
A program may use at most 64 MiB of HBM per device.

v0:
```python
import functools
import math

import jax
import jax.numpy as jnp
from jax import lax
from jax.experimental import pallas as pl
from jax.experimental.pallas import tpu as pltpu
from jax.sharding import Mesh, PartitionSpec as P

LANES = 128
MESH_AXES = ("z", "far_y", "y", "c", "x")
SCATTER = ("c", "x", "y")
SUM = ("z", "far_y")
NEAR_Y = 4
VMEM_LIMIT = 40 * 1024 * 1024
WIDE_LIMIT = 61 * 1024 * 1024
VMEM = pl.BlockSpec(memory_space=pltpu.VMEM)
SMEM = pl.BlockSpec(memory_space=pltpu.SMEM)
HBM = pl.BlockSpec(memory_space=pltpu.HBM)
ROWS = (((1,), (0,)), ((), ()))
COLS = (((1,), (1,)), ((), ()))


def dot(a, b, dims=ROWS):
    return lax.dot_general(a, b, dims, preferred_element_type=jnp.float32)


def activate(pre, cot, keep):
    sig = 0.5 * jnp.tanh(0.5 * pre) + 0.5
    value = keep * (pre * sig)
    slope = (keep * cot.astype(jnp.float32)) * (sig * (1.0 + pre * (1.0 - sig)))
    return value.astype(jnp.bfloat16), slope.astype(jnp.bfloat16)


def taps_of(frames, t, size):
    return jnp.concatenate([rows_of(frames[t - tap : t - tap + size]) for tap in range(3)], 1)


def rows_of(frames):
    return frames.reshape(-1, frames.shape[-1])


def body_kernel(
    length_ref, frames_hbm, cot_hbm, w_hbm, out_hbm, grad, wsum_ref, first_ref,
    frames, cot, w, out, flipped, in_sem, cot_sem, w_sem, out_sem,
):
    count, pixels, width = frames.shape
    middle = 2 + (count - 2) // 2
    groups = [(2, middle), (middle, count)]
    copies = []
    for g, (start, end) in enumerate(groups):
        part = pl.ds(0 if g == 0 else start, end if g == 0 else end - start)
        pair = []
        for source, target, sem in ((frames_hbm, frames, in_sem), (cot_hbm, cot, cot_sem)):
            pair.append(pltpu.make_async_copy(source.at[part], target.at[part], sem.at[g]))
        copies.append(pair)
    w_in = pltpu.make_async_copy(w_hbm, w, w_sem)
    copies[0][0].start()
    w_in.start()
    copies[0][1].start()
    copies[1][0].start()
    copies[1][1].start()
    copies[0][0].wait()
    w_in.wait()
    stacked = rows_of(w[...])
    pre = [dot(taps_of(frames, 2, middle - 2), stacked)]
    copies[0][1].wait()
    copies[1][0].wait()
    pre.append(dot(taps_of(frames, middle, count - middle), stacked))
    copies[1][1].wait()
    for t in range(count):
        flipped[:, t * pixels : (t + 1) * pixels] = frames[t].T
    left = frames_left(length_ref, count)
    done = []
    for g, (start, end) in enumerate(groups):
        slopes = []
        for t in range(start, end):
            rows = slice((t - start) * pixels, (t - start + 1) * pixels)
            keep = (t < left).astype(jnp.float32)
            value, slope = activate(pre[g][rows], cot[t], keep)
            out[t] = value
            grad[t] = slope
            slopes.append(slope)
        part = pl.ds(start, end - start)
        done.append(pltpu.make_async_copy(out.at[part], out_hbm.at[part], out_sem.at[g]))
        done[-1].start()
        slope = jnp.concatenate(slopes, 0)
        for tap in range(3):
            term = dot(flipped[:, (start - tap) * pixels : (end - tap) * pixels], slope)
            part = slice(tap * width, (tap + 1) * width)
            wsum_ref[part, :] = term if g == 0 else wsum_ref[part, :] + term
    first_ref[:2] = frames[:2]
    first_ref[2:] = cot[:2]
    for copy in done:
        copy.wait()


def frames_left(length_ref, count):
    return length_ref[0] - lax.axis_index("x") * count


def piece_at(piece, rows):
    row, col = divmod(piece, 2)
    return slice(row * rows, (row + 1) * rows), slice(col * LANES, (col + 1) * LANES)


def head_kernel(
    scale, count, length_ref, halo, first, w, wpart, out_in, out_hbm, head_ref, terms_ref,
    out, total, out_sem,
):
    del out_in
    pixels, width = halo.shape[1:]
    left = frames_left(length_ref, count)
    back = [halo[0], halo[1], first[0], first[1]]
    lines = [jnp.concatenate(back[2 - tap : 4 - tap], 0) for tap in range(3)]
    pre = dot(jnp.concatenate(lines, 1), rows_of(w[...]))
    flipped = [frame.T for frame in back]
    slopes = []
    for t in range(2):
        keep = (t < left).astype(jnp.float32)
        value, slope = activate(pre[t * pixels : (t + 1) * pixels], first[2 + t], keep)
        out[t] = value
        head_ref[t] = slope
        slopes.append(slope)
    slope = jnp.concatenate(slopes, 0)
    out_copy = pltpu.make_async_copy(out, out_hbm.at[pl.ds(0, 2)], out_sem)
    out_copy.start()
    for tap in range(3):
        part = slice(tap * width, (tap + 1) * width)
        term = dot(jnp.concatenate([flipped[2 - tap], flipped[3 - tap]], 1), slope)
        total[part, :] = (wpart[part, :] + term) * scale
    pieces, rows, _ = terms_ref.shape
    for piece in range(pieces):
        terms_ref[piece] = total[piece_at(piece, rows)].astype(jnp.bfloat16)
    out_copy.wait()


def back_kernel(grad, head, halo, w, out_hbm, out, out_sem):
    count, pixels, width = out.shape
    weights = jnp.concatenate([w[tap].T for tap in range(3)], 0)
    size = 3
    for start in range(0, count, size):
        end = min(start + size, count)
        lines = []
        for tap in range(3):
            picked = []
            for t in range(start + tap, end + tap):
                picked.append(head[t] if t < 2 else grad[t] if t < count else halo[t - count])
            lines.append(jnp.concatenate(picked, 0))
        total = dot(jnp.concatenate(lines, 1), weights)
        out[start:end] = total.astype(jnp.bfloat16).reshape(end - start, pixels, width)
        part = pl.ds(start, end - start)
        pltpu.make_async_copy(out.at[part], out_hbm.at[part], out_sem.at[start // size]).start()
    for start in range(0, count, size):
        part = pl.ds(start, min(size, count - start))
        pltpu.make_async_copy(out.at[part], out_hbm.at[part], out_sem.at[start // size]).wait()


def spread_sum_kernel(in_ref, passed_in, out_ref, passed_out):
    del passed_in, passed_out
    total = jnp.sum(in_ref[...].astype(jnp.float32), 0).astype(jnp.bfloat16)
    for piece in range(out_ref.shape[0]):
        out_ref[piece] = total


def last_kernel(in_ref, out_ref):
    pieces, rows, _ = in_ref.shape
    for piece in range(pieces):
        out_ref[piece_at(piece, rows)] = in_ref[piece].astype(jnp.float32)


def call(kernel, out_shape, in_specs, out_specs, scratch=(), aliases={}, flops=0, moved=0, limit=VMEM_LIMIT):
    return pl.pallas_call(
        kernel,
        out_shape=out_shape,
        in_specs=in_specs,
        out_specs=out_specs,
        scratch_shapes=list(scratch),
        input_output_aliases=aliases,
        compiler_params=pltpu.CompilerParams(vmem_limit_bytes=limit),
        cost_estimate=pl.CostEstimate(flops=flops, bytes_accessed=moved, transcendentals=0),
    )


def passed_along(value, axis, steps):
    count = lax.axis_size(axis)
    first, last = (max(0, -steps), min(count, count - steps))
    return lax.ppermute(value, axis, [(source, source + steps) for source in range(first, last)])


def exchange(value, axes):
    return lax.all_to_all(value, axes, 0, 0, tiled=True)


def spread_sum(terms, passed, copies):
    sds = jax.ShapeDtypeStruct
    shapes = (sds((copies,) + terms.shape[1:], terms.dtype), sds(passed.shape, passed.dtype))
    anywhere = pl.BlockSpec(memory_space=pl.ANY)
    return call(spread_sum_kernel, shapes, [VMEM, anywhere], (VMEM, anywhere), aliases={1: 1})(terms, passed)


def local(lengths, frames, weights, cotangent):
    bf16, f32 = jnp.bfloat16, jnp.float32
    clip, cot = frames[0], cotangent[0]
    count, pixels, chans = clip.shape
    frame = (count, pixels, chans)
    sds = jax.ShapeDtypeStruct
    dma = pltpu.SemaphoreType.DMA
    halo = passed_along(clip[count - 2 :], "x", 1)
    size = pixels * chans * 2
    work = 2 * pixels * chans * chans
    output, grad, wpart, first = call(
        body_kernel,
        (sds(frame, bf16), sds(frame, bf16), sds((3 * chans, chans), f32), sds((4, pixels, chans), bf16)),
        [SMEM, HBM, HBM, HBM],
        (HBM, VMEM, VMEM, VMEM),
        scratch=[
            pltpu.VMEM(frame, bf16),
            pltpu.VMEM(frame, bf16),
            pltpu.VMEM((3, chans, chans), bf16),
            pltpu.VMEM(frame, bf16),
            pltpu.VMEM((chans, count * pixels), bf16),
            dma((2,)),
            dma((2,)),
            dma,
            dma((2,)),
        ],
        flops=(count - 2) * 6 * work,
        moved=36 * size,
        limit=WIDE_LIMIT,
    )(lengths, clip, cot, weights)
    total_rows = lax.axis_size(MESH_AXES) * count * pixels
    pieces, terms_of = lax.axis_size(SCATTER), lax.axis_size(SUM)
    output, head, terms = call(
        functools.partial(head_kernel, 1.0 / math.sqrt(total_rows), count),
        (
            sds(frame, bf16),
            sds((2, pixels, chans), bf16),
            sds((pieces, 3 * chans * chans // LANES // pieces, LANES), bf16),
        ),
        [SMEM, VMEM, VMEM, VMEM, VMEM, HBM],
        (HBM, VMEM, VMEM),
        scratch=[
            pltpu.VMEM((2, pixels, chans), bf16),
            pltpu.VMEM((3 * chans, chans), f32),
            dma,
        ],
        aliases={5: 0},
        flops=12 * work,
        moved=16 * size,
    )(lengths, halo, first, weights, wpart, output)

    terms, head = spread_sum(exchange(terms, SCATTER), head, terms_of)
    following = passed_along(head, "x", -1)
    terms, following = spread_sum(exchange(terms, SUM), following, pieces)
    terms = exchange(terms, SCATTER)
    input_grad = call(
        back_kernel,
        sds(frame, bf16),
        [VMEM, VMEM, VMEM, VMEM],
        HBM,
        scratch=[pltpu.VMEM(frame, bf16), dma((-(-count // 3),))],
        flops=count * 3 * work,
        moved=22 * size,
    )(grad, head, following, weights)
    weight_grad = call(last_kernel, sds((3 * chans, chans), f32), [VMEM], VMEM)(terms)
    return (output[None], input_grad[None], weight_grad.reshape(3, chans, chans))


def solution(mesh):
    dp, tm = mesh.devices.shape
    side = math.isqrt(dp // 2)
    fine = Mesh(mesh.devices.reshape(side, side // NEAR_Y, NEAR_Y, 2, tm), MESH_AXES)
    data = P(MESH_AXES[:4], "x", None, None)
    in_specs = (P(MESH_AXES[:4]), data, P(), data)
    out_specs = (data, data, P())
    return jax.shard_map(local, mesh=fine, in_specs=in_specs, out_specs=out_specs, check_vma=False)
```

profile of v0, /device:TPU:1, one launch (start us, length us, event | category | flops | bytes accessed | tf_op | source)
XLA Modules:
  0.0 85.4 jit_solution(13901452753105409382)
XLA Ops:
  0.6 1.0 %slice_bitcast_fusion = bf16[2,256,256]{2,1,0:T(8,128)(2,1)S(1)} fusion(bf16[1,9,256,256]{3,2,1,0:T(8,128)(2,1)} %param.5), kind=kLoop, calls=%fused_computation | loop fusion | bytes 524288 | tf_op jit(solution)/shard_map/slice | solution.py:210
  1.6 4.0 %collective-permute-start = (bf16[2,256,256]{2,1,0:T(8,128)(2,1)S(1)}, bf16[2,256,256]{2,1,0:T(8,128)(2,1)S(1)}, u32[]{:S(2)}, u32[]{:S(2)}) collective-permute-start(bf16[2,256,256]{2,1,0:T(8,128)(2,1)S(1)} %slice_bitcast_fusion), channel_id=1, source_target_pairs={{0,1},{1,2},{2,3},{4,5},{5,6},{6,7},{8,9},{9,10},{10,11},{12,13},{... | collective-permute-start | bytes 786440 | tf_op jit(solution)/shard_map/ppermute | solution.py:189
  6.2 0.0 copy-start.2
  6.2 6.9 %shard_map.67 = (bf16[9,256,256]{2,1,0:T(8,128)(2,1)}, bf16[9,256,256]{2,1,0:T(8,128)(2,1)}, f32[768,256]{1,0:T(8,128)}, bf16[4,256,256]{2,1,0:T(8,128)(2,1)}) custom-call(s32[1]{0:T(128)S(6)} %copy.13.length_ref, bf16[9,256,256]{2,1,0:T(8,128)(2,1)} %bitcast.9, bf16[9,256,256]{2,1,0:T(8,128)(2,1)} %bitcast.10, bf16[3,256,256]{2,1,0:T(8,128)(2,1)} %w.3), custom_call_target="tpu_custom_call" | custom-call | flops 1409286144 | bytes 4718592 | tf_op jit(solution)/shard_map/pallas_call | solution.py:213
  13.2 0.0 collective-permute-done.halo
  13.2 0.0 copy-done.2
  13.2 0.0 copy-start
  13.2 1.1 %copy-done = f32[768,256]{1,0:T(8,128)S(1)} copy-done((f32[768,256]{1,0:T(8,128)S(1)}, f32[768,256]{1,0:T(8,128)}, u32[]{:S(2)}) %copy-start) | copy-done | bytes 786456
  14.3 0.0 copy-start.1
  14.3 1.0 %copy-done.1 = bf16[4,256,256]{2,1,0:T(8,128)(2,1)S(1)} copy-done((bf16[4,256,256]{2,1,0:T(8,128)(2,1)S(1)}, bf16[4,256,256]{2,1,0:T(8,128)(2,1)}, u32[]{:S(2)}) %copy-start.1) | copy-done | bytes 524312
  15.4 1.4 %shard_map.68 = (bf16[9,256,256]{2,1,0:T(8,128)(2,1)}, bf16[2,256,256]{2,1,0:T(8,128)(2,1)S(1)}, bf16[32,48,128]{2,1,0:T(8,128)(2,1)S(1)}) custom-call(s32[1]{0:T(128)S(6)} %copy.13.length_ref, bf16[2,256,256]{2,1,0:T(8,128)(2,1)S(1)} %collective-permute-done.halo, bf16[4,256,256]{2,1,0:T(8,128)(2,1)S(1)} %copy-done.1, ...), custom_call_target="tpu_custom_call", output_to_operand_aliasing={{0}: (5, {})} | custom-call | flops 402653184 | bytes 2097152 | tf_op jit(solution)/shard_map/pallas_call | solution.py:235
  16.8 20.9 %all_to_all.15.in_ref = bf16[32,48,128]{2,1,0:T(8,128)(2,1)S(1)} all-to-all(bf16[32,48,128]{2,1,0:T(8,128)(2,1)S(1)} %get-tuple-element.19), channel_id=1, replica_groups=mesh['z'=8,'far_y'=2,'y'=4,'c'=2,'x'=4] {'c','x','y'}, dimensions={0} | all-to-all | bytes 786432 | tf_op jit(solution)/shard_map/all_to_all | solution.py:193
  37.7 0.0 copy-start.3
  37.7 0.7 shard_map.69
  38.4 12.7 %all-to-all-start.1 = ((bf16[16,48,128]{2,1,0:T(8,128)(2,1)}), bf16[16,48,128]{2,1,0:T(8,128)(2,1)S(1)}, u32[]{:S(2)}, u32[]{:S(2)}) async-start(bf16[16,48,128]{2,1,0:T(8,128)(2,1)} %get-tuple-element.22), calls=%async_computation.1 | async-start | bytes 393216 | tf_op jit(solution)/shard_map/all_to_all | solution.py:193
  51.2 1.3 %collective-permute-start.1 = (bf16[2,256,256]{2,1,0:T(8,128)(2,1)S(1)}, bf16[2,256,256]{2,1,0:T(8,128)(2,1)S(1)}, u32[]{:S(2)}, u32[]{:S(2)}) collective-permute-start(bf16[2,256,256]{2,1,0:T(8,128)(2,1)S(1)} %get-tuple-element.21.head), channel_id=1, source_target_pairs={{1,0},{2,1},{3,2},{5,4},{6,5},{7,6},{9,8},{10,9},{11,10},{13,12},{... | collective-permute-start | bytes 786440 | tf_op jit(solution)/shard_map/ppermute | solution.py:189
  52.5 6.9 %collective-permute-done.1.passed_in = bf16[2,256,256]{2,1,0:T(8,128)(2,1)S(1)} collective-permute-done((bf16[2,256,256]{2,1,0:T(8,128)(2,1)S(1)}, bf16[2,256,256]{2,1,0:T(8,128)(2,1)S(1)}, u32[]{:S(2)}, u32[]{:S(2)}) %collective-permute-start.1) | collective-permute-done | bytes 262176 | tf_op jit(solution)/shard_map/ppermute | solution.py:189
  59.4 4.0 %all-to-all-done.1.in_ref = bf16[16,48,128]{2,1,0:T(8,128)(2,1)S(1)} async-done(((bf16[16,48,128]{2,1,0:T(8,128)(2,1)}), bf16[16,48,128]{2,1,0:T(8,128)(2,1)S(1)}, u32[]{:S(2)}, u32[]{:S(2)}) %all-to-all-start.1) | async-done | bytes 196640 | tf_op jit(solution)/shard_map/all_to_all | solution.py:193
  63.4 0.8 shard_map.70
  64.2 7.3 %all-to-all-start.2 = ((bf16[32,48,128]{2,1,0:T(8,128)(2,1)}), bf16[32,48,128]{2,1,0:T(8,128)(2,1)S(1)}, u32[]{:S(2)}, u32[]{:S(2)}) async-start(bf16[32,48,128]{2,1,0:T(8,128)(2,1)} %get-tuple-element.24), calls=%async_computation.2 | async-start | bytes 786432 | tf_op jit(solution)/shard_map/all_to_all | solution.py:193
  71.4 0.0 copy-done.3
  71.5 2.1 %shard_map.71 = bf16[9,256,256]{2,1,0:T(8,128)(2,1)} custom-call(bf16[9,256,256]{2,1,0:T(8,128)(2,1)S(1)} %copy-done.3, bf16[2,256,256]{2,1,0:T(8,128)(2,1)S(1)} %get-tuple-element.21.head, bf16[2,256,256]{2,1,0:T(8,128)(2,1)S(1)} %get-tuple-element.23.halo, bf16[3,256,256]{2,1,0:T(8,128)(2,1)S(1)} %copy-done.2), custom_call_target="tpu_custom_call" | custom-call | flops 905969664 | bytes 2883584 | tf_op jit(solution)/shard_map/pallas_call | solution.py:258
  73.5 10.9 %all-to-all-done.2.in_ref = bf16[32,48,128]{2,1,0:T(8,128)(2,1)S(1)} async-done(((bf16[32,48,128]{2,1,0:T(8,128)(2,1)}), bf16[32,48,128]{2,1,0:T(8,128)(2,1)S(1)}, u32[]{:S(2)}, u32[]{:S(2)}) %all-to-all-start.2) | async-done | bytes 393248 | tf_op jit(solution)/shard_map/all_to_all | solution.py:193
  84.4 0.9 %shard_map.72 = f32[768,256]{1,0:T(8,128)} custom-call(bf16[32,48,128]{2,1,0:T(8,128)(2,1)S(1)} %all-to-all-done.2.in_ref), custom_call_target="tpu_custom_call" | custom-call | tf_op jit(solution)/shard_map/pallas_call | solution.py:267
Async XLA Ops:
  1.6 11.6 %collective-permute-start = (bf16[2,256,256]{2,1,0:T(8,128)(2,1)S(1)}, bf16[2,256,256]{2,1,0:T(8,128)(2,1)S(1)}, u32[]{:S(2)}, u32[]{:S(2)}) collective-permute-start(bf16[2,256,256]{2,1,0:T(8,128)(2,1)S(1)} %slice_bitcast_fusion), channel_id=1, source_target_pairs={{0,1},{1,2},{2,3},{4,5},{5,6},{6,7},{8,9},{9,10},{10,11},{12,13},{... | collective-permute-start | bytes 786440 | tf_op jit(solution)/shard_map/ppermute | solution.py:189
  6.2 7.0 %copy-start.2 = (bf16[3,256,256]{2,1,0:T(8,128)(2,1)S(1)}, bf16[3,256,256]{2,1,0:T(8,128)(2,1)}, u32[]{:S(2)}) copy-start(bf16[3,256,256]{2,1,0:T(8,128)(2,1)} %w.3) | copy-start | bytes 1179652
  13.2 1.1 %copy-start = (f32[768,256]{1,0:T(8,128)S(1)}, f32[768,256]{1,0:T(8,128)}, u32[]{:S(2)}) copy-start(f32[768,256]{1,0:T(8,128)} %get-tuple-element.15.wpart) | copy-start | bytes 2359300
  14.3 1.0 %copy-start.1 = (bf16[4,256,256]{2,1,0:T(8,128)(2,1)S(1)}, bf16[4,256,256]{2,1,0:T(8,128)(2,1)}, u32[]{:S(2)}) copy-start(bf16[4,256,256]{2,1,0:T(8,128)(2,1)} %get-tuple-element.14.first) | copy-start | bytes 1572868
  37.7 33.8 %copy-start.3 = (bf16[9,256,256]{2,1,0:T(8,128)(2,1)S(1)}, bf16[9,256,256]{2,1,0:T(8,128)(2,1)}, u32[]{:S(2)}) copy-start(bf16[9,256,256]{2,1,0:T(8,128)(2,1)} %get-tuple-element.18.grad) | copy-start | bytes 3538948
  38.4 24.9 %all-to-all-start.1 = ((bf16[16,48,128]{2,1,0:T(8,128)(2,1)}), bf16[16,48,128]{2,1,0:T(8,128)(2,1)S(1)}, u32[]{:S(2)}, u32[]{:S(2)}) async-start(bf16[16,48,128]{2,1,0:T(8,128)(2,1)} %get-tuple-element.22), calls=%async_computation.1 | async-start | bytes 393216 | tf_op jit(solution)/shard_map/all_to_all | solution.py:193
  51.2 8.2 %collective-permute-start.1 = (bf16[2,256,256]{2,1,0:T(8,128)(2,1)S(1)}, bf16[2,256,256]{2,1,0:T(8,128)(2,1)S(1)}, u32[]{:S(2)}, u32[]{:S(2)}) collective-permute-start(bf16[2,256,256]{2,1,0:T(8,128)(2,1)S(1)} %get-tuple-element.21.head), channel_id=1, source_target_pairs={{1,0},{2,1},{3,2},{5,4},{6,5},{7,6},{9,8},{10,9},{11,10},{13,12},{... | collective-permute-start | bytes 786440 | tf_op jit(solution)/shard_map/ppermute | solution.py:189
  64.2 20.3 %all-to-all-start.2 = ((bf16[32,48,128]{2,1,0:T(8,128)(2,1)}), bf16[32,48,128]{2,1,0:T(8,128)(2,1)S(1)}, u32[]{:S(2)}, u32[]{:S(2)}) async-start(bf16[32,48,128]{2,1,0:T(8,128)(2,1)} %get-tuple-element.24), calls=%async_computation.2 | async-start | bytes 786432 | tf_op jit(solution)/shard_map/all_to_all | solution.py:193
where the time goes:
time: 85.8 us; the launch traced here: 85.4 us
  starting transfers between devices  25.2 us (29%)
  waiting for transfers between devices  21.8 us (25%)
  blocking collectives  20.9 us (24%)
  Pallas kernels  12.8 us (15%)
  local copies, waits for them, and re-layouts  3.15 us (4%)
  between operations  1.38 us (2%)
    all_to_all x1, blocking collectives, exchange(): return lax.all_to_all(value, axes, 0, 0, tiled=True)  20.9 us
    all_to_all x2, starting transfers between devices, exchange(): return lax.all_to_all(value, axes, 0, 0, tiled=True)  20 us
    all_to_all x2, waiting for transfers between devices, exchange(): return lax.all_to_all(value, axes, 0, 0, tiled=True)  14.9 us
    pallas_call x1, Pallas kernels, local(): call(body_kernel, (sds(frame, bf16), sds(frame, bf16), sds((3 * chans, ch...  6.94 us
    ppermute x2, waiting for transfers between devices, passed_along(): lax.ppermute(value, axis, [(source, source + steps) for source in range(f...  6.9 us
    ppermute x2, starting transfers between devices, passed_along(): lax.ppermute(value, axis, [(source, source + steps) for source in range(f...  5.25 us
    unnamed x8, local copies, waits for them, and re-layouts  2.18 us
    pallas_call x1, Pallas kernels, local(): call(back_kernel, sds(frame, bf16), [VMEM, VMEM, VMEM, VMEM], HBM, scratc...  2.05 us
  transfers between devices with their start and end apart: 4, of which 3 were waited for; matrix products, arithmetic and copies ran while one was open for 0% of the time, Pallas kernels for 11%

commit v1 on v0

--- a/solution.py
+++ b/solution.py
@@ -9,12 +9,10 @@
 from jax.sharding import Mesh, PartitionSpec as P
 
 LANES = 128
-MESH_AXES = ("z", "far_y", "y", "c", "x")
-SCATTER = ("c", "x", "y")
-SUM = ("z", "far_y")
-NEAR_Y = 4
+MESH_AXES = ("far_z", "z", "far_y", "y", "c", "x")
+SCATTER = ("c", "x", "y", "z")
+SUM = ("far_z", "far_y")
 VMEM_LIMIT = 40 * 1024 * 1024
-WIDE_LIMIT = 61 * 1024 * 1024
 VMEM = pl.BlockSpec(memory_space=pltpu.VMEM)
 SMEM = pl.BlockSpec(memory_space=pltpu.SMEM)
 HBM = pl.BlockSpec(memory_space=pltpu.HBM)
@@ -41,34 +39,13 @@
     return frames.reshape(-1, frames.shape[-1])
 
 
-def body_kernel(
-    length_ref, frames_hbm, cot_hbm, w_hbm, out_hbm, grad, wsum_ref, first_ref,
-    frames, cot, w, out, flipped, in_sem, cot_sem, w_sem, out_sem,
-):
+def body_kernel(length_ref, frames, cot, w, out_hbm, grad, wsum_ref, out, flipped, out_sem):
     count, pixels, width = frames.shape
     middle = 2 + (count - 2) // 2
     groups = [(2, middle), (middle, count)]
-    copies = []
-    for g, (start, end) in enumerate(groups):
-        part = pl.ds(0 if g == 0 else start, end if g == 0 else end - start)
-        pair = []
-        for source, target, sem in ((frames_hbm, frames, in_sem), (cot_hbm, cot, cot_sem)):
-            pair.append(pltpu.make_async_copy(source.at[part], target.at[part], sem.at[g]))
-        copies.append(pair)
-    w_in = pltpu.make_async_copy(w_hbm, w, w_sem)
-    copies[0][0].start()
-    w_in.start()
-    copies[0][1].start()
-    copies[1][0].start()
-    copies[1][1].start()
-    copies[0][0].wait()
-    w_in.wait()
     stacked = rows_of(w[...])
     pre = [dot(taps_of(frames, 2, middle - 2), stacked)]
-    copies[0][1].wait()
-    copies[1][0].wait()
     pre.append(dot(taps_of(frames, middle, count - middle), stacked))
-    copies[1][1].wait()
     for t in range(count):
         flipped[:, t * pixels : (t + 1) * pixels] = frames[t].T
     left = frames_left(length_ref, count)
@@ -90,8 +67,6 @@
             term = dot(flipped[:, (start - tap) * pixels : (end - tap) * pixels], slope)
             part = slice(tap * width, (tap + 1) * width)
             wsum_ref[part, :] = term if g == 0 else wsum_ref[part, :] + term
-    first_ref[:2] = frames[:2]
-    first_ref[2:] = cot[:2]
     for copy in done:
         copy.wait()
 
@@ -106,20 +81,20 @@
 
 
 def head_kernel(
-    scale, count, length_ref, halo, first, w, wpart, out_in, out_hbm, head_ref, terms_ref,
+    scale, count, length_ref, halo, frames, cot, w, wpart, out_in, out_hbm, head_ref, terms_ref,
     out, total, out_sem,
 ):
     del out_in
     pixels, width = halo.shape[1:]
     left = frames_left(length_ref, count)
-    back = [halo[0], halo[1], first[0], first[1]]
+    back = [halo[0], halo[1], frames[0], frames[1]]
     lines = [jnp.concatenate(back[2 - tap : 4 - tap], 0) for tap in range(3)]
     pre = dot(jnp.concatenate(lines, 1), rows_of(w[...]))
     flipped = [frame.T for frame in back]
     slopes = []
     for t in range(2):
         keep = (t < left).astype(jnp.float32)
-        value, slope = activate(pre[t * pixels : (t + 1) * pixels], first[2 + t], keep)
+        value, slope = activate(pre[t * pixels : (t + 1) * pixels], cot[t], keep)
         out[t] = value
         head_ref[t] = slope
         slopes.append(slope)
@@ -157,8 +132,8 @@
         pltpu.make_async_copy(out.at[part], out_hbm.at[part], out_sem.at[start // size]).wait()
 
 
-def spread_sum_kernel(in_ref, passed_in, out_ref, passed_out):
-    del passed_in, passed_out
+def spread_sum_kernel(in_ref, *refs):
+    out_ref = refs[-1]
     total = jnp.sum(in_ref[...].astype(jnp.float32), 0).astype(jnp.bfloat16)
     for piece in range(out_ref.shape[0]):
         out_ref[piece] = total
@@ -170,7 +145,7 @@
         out_ref[piece_at(piece, rows)] = in_ref[piece].astype(jnp.float32)
 
 
-def call(kernel, out_shape, in_specs, out_specs, scratch=(), aliases={}, flops=0, moved=0, limit=VMEM_LIMIT):
+def call(kernel, out_shape, in_specs, out_specs, scratch=(), aliases={}, flops=0, moved=0):
     return pl.pallas_call(
         kernel,
         out_shape=out_shape,
@@ -178,7 +153,7 @@
         out_specs=out_specs,
         scratch_shapes=list(scratch),
         input_output_aliases=aliases,
-        compiler_params=pltpu.CompilerParams(vmem_limit_bytes=limit),
+        compiler_params=pltpu.CompilerParams(vmem_limit_bytes=VMEM_LIMIT),
         cost_estimate=pl.CostEstimate(flops=flops, bytes_accessed=moved, transcendentals=0),
     )
 
@@ -193,11 +168,15 @@
     return lax.all_to_all(value, axes, 0, 0, tiled=True)
 
 
-def spread_sum(terms, passed, copies):
+def spread_sum(terms, copies, *passed):
     sds = jax.ShapeDtypeStruct
-    shapes = (sds((copies,) + terms.shape[1:], terms.dtype), sds(passed.shape, passed.dtype))
-    anywhere = pl.BlockSpec(memory_space=pl.ANY)
-    return call(spread_sum_kernel, shapes, [VMEM, anywhere], (VMEM, anywhere), aliases={1: 1})(terms, passed)
+    shapes = [sds(value.shape, value.dtype) for value in passed]
+    shapes.append(sds((copies,) + terms.shape[1:], terms.dtype))
+    anywhere = [pl.BlockSpec(memory_space=pl.ANY)] * len(passed)
+    aliases = {i + 1: i for i in range(len(passed))}
+    return call(spread_sum_kernel, shapes, [VMEM] + anywhere, anywhere + [VMEM], aliases=aliases)(
+        terms, *passed
+    )
 
 
 def local(lengths, frames, weights, cotangent):
@@ -210,25 +189,14 @@
     halo = passed_along(clip[count - 2 :], "x", 1)
     size = pixels * chans * 2
     work = 2 * pixels * chans * chans
-    output, grad, wpart, first = call(
+    output, grad, wpart = call(
         body_kernel,
-        (sds(frame, bf16), sds(frame, bf16), sds((3 * chans, chans), f32), sds((4, pixels, chans), bf16)),
-        [SMEM, HBM, HBM, HBM],
-        (HBM, VMEM, VMEM, VMEM),
-        scratch=[
-            pltpu.VMEM(frame, bf16),
-            pltpu.VMEM(frame, bf16),
-            pltpu.VMEM((3, chans, chans), bf16),
-            pltpu.VMEM(frame, bf16),
-            pltpu.VMEM((chans, count * pixels), bf16),
-            dma((2,)),
-            dma((2,)),
-            dma,
-            dma((2,)),
-        ],
+        (sds(frame, bf16), sds(frame, bf16), sds((3 * chans, chans), f32)),
+        [SMEM, VMEM, VMEM, VMEM],
+        (HBM, VMEM, VMEM),
+        scratch=[pltpu.VMEM(frame, bf16), pltpu.VMEM((chans, count * pixels), bf16), dma((2,))],
         flops=(count - 2) * 6 * work,
         moved=36 * size,
-        limit=WIDE_LIMIT,
     )(lengths, clip, cot, weights)
     total_rows = lax.axis_size(MESH_AXES) * count * pixels
     pieces, terms_of = lax.axis_size(SCATTER), lax.axis_size(SUM)
@@ -239,21 +207,21 @@
             sds((2, pixels, chans), bf16),
             sds((pieces, 3 * chans * chans // LANES // pieces, LANES), bf16),
         ),
-        [SMEM, VMEM, VMEM, VMEM, VMEM, HBM],
+        [SMEM, VMEM, VMEM, VMEM, VMEM, VMEM, HBM],
         (HBM, VMEM, VMEM),
         scratch=[
             pltpu.VMEM((2, pixels, chans), bf16),
             pltpu.VMEM((3 * chans, chans), f32),
             dma,
         ],
-        aliases={5: 0},
+        aliases={6: 0},
         flops=12 * work,
         moved=16 * size,
-    )(lengths, halo, first, weights, wpart, output)
-
-    terms, head = spread_sum(exchange(terms, SCATTER), head, terms_of)
+    )(lengths, halo, clip, cot, weights, wpart, output)
+
+    head, terms = spread_sum(exchange(terms, SCATTER), terms_of, head)
     following = passed_along(head, "x", -1)
-    terms, following = spread_sum(exchange(terms, SUM), following, pieces)
+    (terms,) = spread_sum(exchange(terms, SUM), pieces)
     terms = exchange(terms, SCATTER)
     input_grad = call(
         back_kernel,
@@ -271,8 +239,8 @@
 def solution(mesh):
     dp, tm = mesh.devices.shape
     side = math.isqrt(dp // 2)
-    fine = Mesh(mesh.devices.reshape(side, side // NEAR_Y, NEAR_Y, 2, tm), MESH_AXES)
-    data = P(MESH_AXES[:4], "x", None, None)
-    in_specs = (P(MESH_AXES[:4]), data, P(), data)
+    fine = Mesh(mesh.devices.reshape(side // 2, 2, -1, 2, 2, tm), MESH_AXES)
+    data = P(MESH_AXES[:5], "x", None, None)
+    in_specs = (P(MESH_AXES[:5]), data, P(), data)
     out_specs = (data, data, P())
     return jax.shard_map(local, mesh=fine, in_specs=in_specs, out_specs=out_specs, check_vma=False)

time: 85.8 us -> 78.9 us (0.920)
  blocking collectives: 20.9 us -> 42.8 us
  starting transfers between devices: 25.2 us -> 11.3 us
  waiting for transfers between devices: 21.8 us -> 11 us
  Pallas kernels: 12.8 us -> 7.55 us
  local copies, waits for them, and re-layouts: 3.15 us -> 4.51 us
    all_to_all x1 -> x2, blocking collectives: 20.9 us -> 42.8 us  [exchange(): return lax.all_to_all(value, axes, 0, 0, tiled=True)]
    all_to_all x2 -> x1, waiting for transfers between devices: 14.9 us -> 0.01 us  [exchange(): return lax.all_to_all(value, axes, 0, 0, tiled=True)]
    all_to_all x2 -> x1, starting transfers between devices: 20 us -> 6.03 us  [exchange(): return lax.all_to_all(value, axes, 0, 0, tiled=True)]
    pallas_call x1, Pallas kernels: 6.94 us -> 2.33 us  [local(): call(body_kernel, (sds(frame, bf16), sds(frame, bf16), sds((3 * chans, ch...]
    ppermute x2, waiting for transfers between devices: 6.9 us -> 11 us  [passed_along(): lax.ppermute(value, axis, [(source, source + steps) for source in range(f...]
    unnamed x8, local copies, waits for them, and re-layouts: 2.18 us -> 3.53 us
  transfers between devices with their start and end apart: 4 -> 3, of which waited for: 3 -> 1; matrix products, arithmetic and copies ran while one was open for 0% -> 0% of each run, Pallas kernels for 11% -> 6%
where the time goes in v1:
time: 78.9 us; the launch traced here: 78.5 us
  blocking collectives  42.8 us (54%)
  starting transfers between devices  11.3 us (14%)
  waiting for transfers between devices  11 us (14%)
  Pallas kernels  7.55 us (10%)
  local copies, waits for them, and re-layouts  4.51 us (6%)
  between operations  1.36 us (2%)
    all_to_all x2, blocking collectives, exchange(): return lax.all_to_all(value, axes, 0, 0, tiled=True)  42.8 us
    ppermute x2, waiting for transfers between devices, passed_along(): lax.ppermute(value, axis, [(source, source + steps) for source in range(f...  11 us
    all_to_all x1, starting transfers between devices, exchange(): return lax.all_to_all(value, axes, 0, 0, tiled=True)  6.03 us
    ppermute x2, starting transfers between devices, passed_along(): lax.ppermute(value, axis, [(source, source + steps) for source in range(f...  5.25 us
    unnamed x8, local copies, waits for them, and re-layouts  3.53 us
    pallas_call x1, Pallas kernels, local(): call(body_kernel, (sds(frame, bf16), sds(frame, bf16), sds((3 * chans, ch...  2.33 us
    pallas_call x1, Pallas kernels, local(): call(back_kernel, sds(frame, bf16), [VMEM, VMEM, VMEM, VMEM], HBM, scratc...  2.05 us
  transfers between devices with their start and end apart: 3, of which 1 were waited for; matrix products, arithmetic and copies ran while one was open for 0% of the time, Pallas kernels for 6%

profile of v1, /device:TPU:1, one launch (start us, length us, event | category | flops | bytes accessed | tf_op | source)
XLA Modules:
  0.0 78.5 jit_solution(15695626425129355610)
XLA Ops:
  0.6 1.0 %slice_bitcast_fusion = bf16[2,256,256]{2,1,0:T(8,128)(2,1)S(1)} fusion(bf16[1,9,256,256]{3,2,1,0:T(8,128)(2,1)} %param.5), kind=kLoop, calls=%fused_computation | loop fusion | bytes 524288 | tf_op jit(solution)/shard_map/slice | solution.py:189
  1.6 4.0 %collective-permute-start = (bf16[2,256,256]{2,1,0:T(8,128)(2,1)S(1)}, bf16[2,256,256]{2,1,0:T(8,128)(2,1)S(1)}, u32[]{:S(2)}, u32[]{:S(2)}) collective-permute-start(bf16[2,256,256]{2,1,0:T(8,128)(2,1)S(1)} %slice_bitcast_fusion), channel_id=1, source_target_pairs={{0,1},{1,2},{2,3},{4,5},{5,6},{6,7},{8,9},{9,10},{10,11},{12,13},{... | collective-permute-start | bytes 786440 | tf_op jit(solution)/shard_map/ppermute | solution.py:164
  6.2 0.0 copy-start
  6.2 1.3 %copy-done = bf16[1,9,256,256]{3,2,1,0:T(8,128)(2,1)S(1)} copy-done((bf16[1,9,256,256]{3,2,1,0:T(8,128)(2,1)S(1)}, bf16[1,9,256,256]{3,2,1,0:T(8,128)(2,1)}, u32[]{:S(2)}) %copy-start) | copy-done | bytes 1179672
  7.5 0.0 copy-start.1
  7.5 1.3 %copy-done.1 = bf16[1,9,256,256]{3,2,1,0:T(8,128)(2,1)S(1)} copy-done((bf16[1,9,256,256]{3,2,1,0:T(8,128)(2,1)S(1)}, bf16[1,9,256,256]{3,2,1,0:T(8,128)(2,1)}, u32[]{:S(2)}) %copy-start.1) | copy-done | bytes 1179672
  8.8 0.0 copy-start.2
  8.8 1.0 %copy-done.2 = bf16[3,256,256]{2,1,0:T(8,128)(2,1)S(1)} copy-done((bf16[3,256,256]{2,1,0:T(8,128)(2,1)S(1)}, bf16[3,256,256]{2,1,0:T(8,128)(2,1)}, u32[]{:S(2)}) %copy-start.2) | copy-done | bytes 393240
  9.8 2.3 %shard_map.67 = (bf16[9,256,256]{2,1,0:T(8,128)(2,1)}, bf16[9,256,256]{2,1,0:T(8,128)(2,1)S(1)}, f32[768,256]{1,0:T(8,128)S(1)}) custom-call(s32[1]{0:T(128)S(6)} %copy.11.length_ref, bf16[9,256,256]{2,1,0:T(8,128)(2,1)S(1)} %bitcast.7, bf16[9,256,256]{2,1,0:T(8,128)(2,1)S(1)} %bitcast.9, bf16[3,256,256]{2,1,0:T(8,128)(2,1)S(1)} %copy-done.2), custom_call_target="tpu_custom_call" | custom-call | flops 1409286144 | bytes 4718592 | tf_op jit(solution)/shard_map/pallas_call | solution.py:192
  12.1 0.0 collective-permute-done.halo
  12.1 1.4 %shard_map.68 = (bf16[9,256,256]{2,1,0:T(8,128)(2,1)}, bf16[2,256,256]{2,1,0:T(8,128)(2,1)S(1)}, bf16[32,48,128]{2,1,0:T(8,128)(2,1)S(1)}) custom-call(s32[1]{0:T(128)S(6)} %copy.11.length_ref, bf16[2,256,256]{2,1,0:T(8,128)(2,1)S(1)} %collective-permute-done.halo, bf16[9,256,256]{2,1,0:T(8,128)(2,1)S(1)} %bitcast.8, ...), custom_call_target="tpu_custom_call", output_to_operand_aliasing={{0}: (6, {})} | custom-call | flops 402653184 | bytes 2097152 | tf_op jit(solution)/shard_map/pallas_call | solution.py:203
  13.5 17.5 %all_to_all.15.in_ref = bf16[32,48,128]{2,1,0:T(8,128)(2,1)S(1)} all-to-all(bf16[32,48,128]{2,1,0:T(8,128)(2,1)S(1)} %get-tuple-element.15), channel_id=1, replica_groups=mesh['far_z'=4,'z'=2,'far_y'=4,'y'=2,'c'=2,'x'=4] {'c','x','y','z'}, dimensions={0} | all-to-all | bytes 786432 | tf_op jit(solution)/shard_map/all_to_all | solution.py:168
  31.0 0.0 copy-start.3
  31.0 0.1 shard_map.69
  31.1 25.2 %all_to_all.16.in_ref = bf16[16,48,128]{2,1,0:T(8,128)(2,1)S(1)} all-to-all(bf16[16,48,128]{2,1,0:T(8,128)(2,1)S(1)} %get-tuple-element.18), channel_id=1, replica_groups=mesh['far_z'=4,'z'=2,'far_y'=4,'y'=2,'c'=2,'x'=4] {'far_z','far_y'}, dimensions={0} | all-to-all | bytes 393216 | tf_op jit(solution)/shard_map/all_to_all | solution.py:168
  56.4 0.8 %shard_map.71 = bf16[32,48,128]{2,1,0:T(8,128)(2,1)} custom-call(bf16[16,48,128]{2,1,0:T(8,128)(2,1)S(1)} %all_to_all.16.in_ref), custom_call_target="tpu_custom_call" | custom-call | tf_op jit(solution)/shard_map/pallas_call | solution.py:177
  57.1 6.0 %all-to-all-start.2 = ((bf16[32,48,128]{2,1,0:T(8,128)(2,1)}), bf16[32,48,128]{2,1,0:T(8,128)(2,1)S(1)}, u32[]{:S(2)}, u32[]{:S(2)}) async-start(bf16[32,48,128]{2,1,0:T(8,128)(2,1)} %shard_map.71), calls=%async_computation.2 | async-start | bytes 786432 | tf_op jit(solution)/shard_map/all_to_all | solution.py:168
  63.2 1.3 %collective-permute-start.1 = (bf16[2,256,256]{2,1,0:T(8,128)(2,1)S(1)}, bf16[2,256,256]{2,1,0:T(8,128)(2,1)S(1)}, u32[]{:S(2)}, u32[]{:S(2)}) collective-permute-start(bf16[2,256,256]{2,1,0:T(8,128)(2,1)S(1)} %get-tuple-element.17.head), channel_id=1, source_target_pairs={{1,0},{2,1},{3,2},{5,4},{6,5},{7,6},{9,8},{10,9},{11,10},{13,12},{... | collective-permute-start | bytes 786440 | tf_op jit(solution)/shard_map/ppermute | solution.py:164
  64.5 11.0 %collective-permute-done.1.halo = bf16[2,256,256]{2,1,0:T(8,128)(2,1)S(1)} collective-permute-done((bf16[2,256,256]{2,1,0:T(8,128)(2,1)S(1)}, bf16[2,256,256]{2,1,0:T(8,128)(2,1)S(1)}, u32[]{:S(2)}, u32[]{:S(2)}) %collective-permute-start.1) | collective-permute-done | bytes 262176 | tf_op jit(solution)/shard_map/ppermute | solution.py:164
  75.5 0.0 copy-done.3
  75.5 2.0 %shard_map.70 = bf16[9,256,256]{2,1,0:T(8,128)(2,1)} custom-call(bf16[9,256,256]{2,1,0:T(8,128)(2,1)S(1)} %get-tuple-element.14.grad, bf16[2,256,256]{2,1,0:T(8,128)(2,1)S(1)} %get-tuple-element.17.head, bf16[2,256,256]{2,1,0:T(8,128)(2,1)S(1)} %collective-permute-done.1.halo, bf16[3,256,256]{2,1,0:T(8,128)(2,1)S(1)} %copy-done.3), custom_call_target="tpu_custom_call" | custom-call | flops 905969664 | bytes 2883584 | tf_op jit(solution)/shard_map/pallas_call | solution.py:226
  77.5 0.0 all-to-all-done.2.in_ref
  77.5 0.9 %shard_map.72 = f32[768,256]{1,0:T(8,128)} custom-call(bf16[32,48,128]{2,1,0:T(8,128)(2,1)S(1)} %all-to-all-done.2.in_ref), custom_call_target="tpu_custom_call" | custom-call | tf_op jit(solution)/shard_map/pallas_call | solution.py:235
Async XLA Ops:
  1.6 10.5 %collective-permute-start = (bf16[2,256,256]{2,1,0:T(8,128)(2,1)S(1)}, bf16[2,256,256]{2,1,0:T(8,128)(2,1)S(1)}, u32[]{:S(2)}, u32[]{:S(2)}) collective-permute-start(bf16[2,256,256]{2,1,0:T(8,128)(2,1)S(1)} %slice_bitcast_fusion), channel_id=1, source_target_pairs={{0,1},{1,2},{2,3},{4,5},{5,6},{6,7},{8,9},{9,10},{10,11},{12,13},{... | collective-permute-start | bytes 786440 | tf_op jit(solution)/shard_map/ppermute | solution.py:164
  6.2 1.3 %copy-start = (bf16[1,9,256,256]{3,2,1,0:T(8,128)(2,1)S(1)}, bf16[1,9,256,256]{3,2,1,0:T(8,128)(2,1)}, u32[]{:S(2)}) copy-start(bf16[1,9,256,256]{3,2,1,0:T(8,128)(2,1)} %param.5) | copy-start | bytes 3538948
  7.5 1.3 %copy-start.1 = (bf16[1,9,256,256]{3,2,1,0:T(8,128)(2,1)S(1)}, bf16[1,9,256,256]{3,2,1,0:T(8,128)(2,1)}, u32[]{:S(2)}) copy-start(bf16[1,9,256,256]{3,2,1,0:T(8,128)(2,1)} %param.7) | copy-start | bytes 3538948
  8.8 1.0 %copy-start.2 = (bf16[3,256,256]{2,1,0:T(8,128)(2,1)S(1)}, bf16[3,256,256]{2,1,0:T(8,128)(2,1)}, u32[]{:S(2)}) copy-start(bf16[3,256,256]{2,1,0:T(8,128)(2,1)} %w.5) | copy-start | bytes 1179652
  31.0 44.4 %copy-start.3 = (bf16[3,256,256]{2,1,0:T(8,128)(2,1)S(1)}, bf16[3,256,256]{2,1,0:T(8,128)(2,1)}, u32[]{:S(2)}) copy-start(bf16[3,256,256]{2,1,0:T(8,128)(2,1)} %w.5) | copy-start | bytes 1179652
  57.1 20.4 %all-to-all-start.2 = ((bf16[32,48,128]{2,1,0:T(8,128)(2,1)}), bf16[32,48,128]{2,1,0:T(8,128)(2,1)S(1)}, u32[]{:S(2)}, u32[]{:S(2)}) async-start(bf16[32,48,128]{2,1,0:T(8,128)(2,1)} %shard_map.71), calls=%async_computation.2 | async-start | bytes 786432 | tf_op jit(solution)/shard_map/all_to_all | solution.py:168
  63.2 12.3 %collective-permute-start.1 = (bf16[2,256,256]{2,1,0:T(8,128)(2,1)S(1)}, bf16[2,256,256]{2,1,0:T(8,128)(2,1)S(1)}, u32[]{:S(2)}, u32[]{:S(2)}) collective-permute-start(bf16[2,256,256]{2,1,0:T(8,128)(2,1)S(1)} %get-tuple-element.17.head), channel_id=1, source_target_pairs={{1,0},{2,1},{3,2},{5,4},{6,5},{7,6},{9,8},{10,9},{11,10},{13,12},{... | collective-permute-start | bytes 786440 | tf_op jit(solution)/shard_map/ppermute | solution.py:164
